TPU v7x, 32 devices: a whole 2x2x4 slice. The times are simulated.
32 devices in a mesh: mx: 8 (over y, x, core), my: 4 (over z).
Axes of the slice: x: 2, y: 2, z: 4, core: 2. Of those that a mesh axis runs over, the one named last changes fastest.
Arguments:
- documents: bfloat16 [32768, 768], P(('mx', 'my')), may hold values from -12 to 12
- owner_tile: int32 [32768, 1], P(('mx', 'my')), may hold values from 0 to 31; in each aligned block of 1024 rows (0 to 1023, 1024 to 2047, ...) at most 64 rows name the same one
- unit_in_tile: int32 [32768], P(('mx', 'my')), may hold values from 0 to 4095
- codebook: bfloat16 [512, 256, 768], P('mx', 'my'), may hold values from -6 to 6
Outputs:
- new_codebook: bfloat16 [512, 256, 768], P('mx', 'my')
Inputs may be any that keep to these rules, and one draw needn't show every extreme that they name: `owner_tile`: among the rows of one device no tile is named by more than 64 documents, and in every draw some tile is named by exactly 64 rows of some device.
All inputs are finite; a program needn't handle non-finite values.
Results may differ from a plain program's by a relative error of at most 0.001.
Values may be sent and summed in bfloat16 or wider, within the bound.
A program may use at most 256 MiB of HBM per device.

v0:
```python
import math

import jax
import jax.numpy as jnp
from jax import lax
from jax.sharding import PartitionSpec as P

RADIUS = 8


def extended(x, sides, width):
    for axis, dim in sides:
        devices, length = (lax.axis_size(axis), x.shape[dim])
        up = [(i, (i + 1) % devices) for i in range(devices - 1)]
        down = [(j, i) for i, j in up]
        last = lax.slice_in_dim(x, length - width, length, axis=dim)
        leading = lax.slice_in_dim(x, 0, width, axis=dim)
        before = lax.ppermute(last, axis, up)
        after = lax.ppermute(leading, axis, down)
        x = jnp.concatenate([before, x, after], axis=dim)
    return x


def smooth_along(values_in, axis_dim, extent):
    weights = [
        math.exp(-2.0 * shift_k * shift_k / RADIUS**2) for shift_k in range(-RADIUS, RADIUS + 1)
    ]
    result = weights[0] * lax.slice_in_dim(values_in, 0, extent, axis=axis_dim)
    for place in range(1, 2 * RADIUS + 1):
        result = result + weights[place] * lax.slice_in_dim(
            values_in, place, place + extent, axis=axis_dim
        )
    return result


def on_device(documents, owner_tile, unit_in_tile, codebook):
    rows_mx = lax.axis_size("mx")
    cols_my = lax.axis_size("my")
    tile_total = rows_mx * cols_my
    rows_tile, cols_tile, feature = codebook.shape
    doc_count = documents.shape[0]
    capacity = max(2, 2 * doc_count // tile_total)
    target = owner_tile[:, 0]
    tile_hits = (target[:, None] == jnp.arange(tile_total, dtype=jnp.int32)[None, :]).astype(
        jnp.int32
    )
    earlier = jnp.cumsum(tile_hits, axis=0) - tile_hits
    slot_pos = jnp.sum(earlier * tile_hits, axis=1)
    unit_row = unit_in_tile // cols_tile
    unit_col = unit_in_tile % cols_tile
    send_place = target * capacity + slot_pos
    outgoing = (
        jnp.zeros((tile_total * capacity, feature), jnp.bfloat16).at[send_place].set(documents)
    )
    unit_mark = jnp.stack([unit_row, unit_col], axis=1).astype(jnp.bfloat16)
    slot_marks = (
        jnp.full((tile_total * capacity, 2), -1.0, jnp.bfloat16).at[send_place].set(unit_mark)
    )
    got_docs, got_marks = (
        lax.all_to_all(
            outgoing.reshape(tile_total, capacity, feature),
            ("mx", "my"),
            split_axis=0,
            concat_axis=0,
            tiled=True,
        ),
        lax.all_to_all(
            slot_marks.reshape(tile_total, capacity, 2),
            ("mx", "my"),
            split_axis=0,
            concat_axis=0,
            tiled=True,
        ),
    )
    received = got_docs.reshape(-1, feature)
    marks_in = got_marks.reshape(-1, 2)
    unit_ids = marks_in[:, 0].astype(jnp.int32) * cols_tile + marks_in[:, 1].astype(jnp.int32)
    row_total = received.shape[0]
    block_rows = min(512, row_total)
    unit_total = rows_tile * cols_tile
    unit_range = jnp.arange(unit_total, dtype=jnp.int32)

    def accumulate(step_i, totals):
        numerator, counter = totals
        offset = step_i * block_rows
        block_docs = lax.dynamic_slice_in_dim(received, offset, block_rows, 0)
        block_ids = lax.dynamic_slice_in_dim(unit_ids, offset, block_rows, 0)
        one_hot = (block_ids[:, None] == unit_range[None, :]).astype(jnp.bfloat16)
        numerator = numerator + lax.dot_general(
            one_hot, block_docs, (((0,), (0,)), ((), ())), preferred_element_type=jnp.float32
        )
        counter = counter + jnp.sum(one_hot, axis=0, dtype=jnp.float32)
        return (numerator, counter)

    start_totals = (
        jnp.zeros((unit_total, feature), jnp.float32),
        jnp.zeros((unit_total,), jnp.float32),
    )
    numerator, counter = lax.fori_loop(0, row_total // block_rows, accumulate, start_totals)
    numerator = numerator.reshape(rows_tile, cols_tile, feature)
    counter = counter.reshape(rows_tile, cols_tile)
    padded_num, padded_hits = (
        extended(numerator, (("mx", 0), ("my", 1)), RADIUS),
        extended(counter, (("mx", 0), ("my", 1)), RADIUS),
    )
    row_num = smooth_along(padded_num, 0, rows_tile)
    row_hits = smooth_along(padded_hits, 0, rows_tile)
    smooth_num = smooth_along(row_num, 1, cols_tile)
    smooth_hits = smooth_along(row_hits, 1, cols_tile)
    updated = (smooth_num + 8.0 * codebook.astype(jnp.float32)) / (smooth_hits[:, :, None] + 8.0)
    return updated.astype(jnp.bfloat16)


def solution(mesh):
    return jax.shard_map(
        on_device,
        mesh=mesh,
        in_specs=(
            P(("mx", "my"), None),
            P(("mx", "my"), None),
            P(("mx", "my")),
            P("mx", "my", None),
        ),
        out_specs=P("mx", "my", None),
        check_vma=False,
    )
```

profile of v0, /device:TPU:12, one launch (start us, length us, event | category | flops | bytes accessed | tf_op | source)
XLA Modules:
  0.0 449.3 jit_solution(15918540711472095987)
XLA Ops:
  0.0 0.7 fusion.47
  0.7 9.0 %reduce-window.6 = s32[32,8,128]{2,1,0:T(8,128)S(1)} reduce-window(s32[32,8,128]{2,1,0:T(8,128)S(1)} %fusion.47, s32[]{:T(128)} %constant.50.clone.1), window={size=1x1x128 pad=0_0x0_0x127_0}, to_apply=%region_0.0 | reduce-window | flops 4161536 | bytes 262148 | tf_op jit(solution)/shard_map/reduce-window
  9.7 0.1 slice.352
  9.8 0.1 copy.20
  10.0 0.1 copy.21
  10.1 0.1 broadcast_add_fusion
  10.2 0.7 fusion.46
  10.9 0.7 compare_select_fusion
  11.6 0.7 fusion.81
  12.3 0.2 copy.22
  12.6 3.3 scatter_custom_fusion
  15.9 0.9 copy.23
  16.8 6.0 %all-to-all-start = ((bf16[32,64,2]{1,2,0:T(2,128)(2,1)}), bf16[32,64,2]{1,2,0:T(2,128)(2,1)S(1)}, u32[]{:S(2)}, u32[]{:S(2)}) async-start(bf16[32,64,2]{1,2,0:T(2,128)(2,1)} %copy.23), calls=%async_computation | async-start | bytes 32768 | tf_op jit(solution)/shard_map/all_to_all | solution.py:67
  22.8 7.9 %scatter_custom_fusion.1 = bf16[2048,768]{1,0:T(8,128)(2,1)} fusion(s32[1024]{0:T(1024)S(1)} %bitcast.45, bf16[1024,768]{1,0:T(8,128)(2,1)} %param.6, bf16[]{:T(256)} %constant.52.clone.1), kind=kCustom, calls=%fused_computation.83 | custom fusion | bytes 3146240 | tf_op jit(solution)/shard_map/scatter | solution.py:53
  30.7 0.0 all-to-all-done
  30.7 5.8 %all-to-all-start.1 = ((bf16[32,64,768]{2,1,0:T(8,128)(2,1)}), bf16[32,64,768]{2,1,0:T(8,128)(2,1)S(1)}, u32[]{:S(2)}, u32[]{:S(2)}) async-start(bf16[32,64,768]{2,1,0:T(8,128)(2,1)} %bitcast.34), calls=%async_computation.1 | async-start | bytes 6291456 | tf_op jit(solution)/shard_map/all_to_all | solution.py:60
  36.5 0.1 reshape.66
  36.7 70.4 %all-to-all-done.1 = bf16[32,64,768]{2,1,0:T(8,128)(2,1)S(1)} async-done(((bf16[32,64,768]{2,1,0:T(8,128)(2,1)}), bf16[32,64,768]{2,1,0:T(8,128)(2,1)S(1)}, u32[]{:S(2)}, u32[]{:S(2)}) %all-to-all-start.1) | async-done | bytes 3145760 | tf_op jit(solution)/shard_map/all_to_all | solution.py:60
  107.0 43.1 %while.16 = (s32[]{:T(128)}, f32[4096,768]{1,0:T(8,128)}, f32[4096]{0:T(1024)S(1)}, s32[2048]{0:T(1024)S(1)}, bf16[2048,768]{1,0:T(8,128)(2,1)S(1)}, /*index=5*/s32[]{:T(128)}, s32[]{:T(128)}, s32[]{:T(128)}, s32[]{:T(128)}) while((s32[]{:T(128)}, f32[4096,768]{1,0:T(8,128)}, f32[4096]{0:T(1024)S(1)}, s32[2048]{0:T(1024)S(1)}, ...), condition=%wide.region_7.8_spmd.clone, body=%wide.region_5.7_spmd.clone.sunk | while | flops 3238006784 | bytes 26026148 | solution.py:99
  107.0 0.1 dynamic_slice.21
  107.1 6.6 %select_add_fusion.4 = f32[4096,768]{1,0:T(8,128)} fusion(f32[4096,768]{1,0:T(8,128)} %get-tuple-element.198, pred[]{:T(512)S(6)} %compare.6, s32[512]{0:T(512)S(1)} %dynamic_slice.21, bf16[2048,768]{1,0:T(8,128)(2,1)S(1)} %get-tuple-element.210, s32[]{:T(128)S(6)} %select_n.37), kind=kOutput, calls=%fused_computation.3.clone.1 | convolution fusion | flops 3229614080 | bytes 25954308 | tf_op jit(solution)/shard_map/while/body/eval_jaxpr/dot_general | solution.py:89
  113.7 2.0 convert_reduce_fusion.2
  115.7 0.1 dynamic_slice.21
  115.8 9.4 %select_add_fusion.4 = f32[4096,768]{1,0:T(8,128)} fusion(f32[4096,768]{1,0:T(8,128)} %get-tuple-element.198, pred[]{:T(512)S(6)} %compare.6, s32[512]{0:T(512)S(1)} %dynamic_slice.21, bf16[2048,768]{1,0:T(8,128)(2,1)S(1)} %get-tuple-element.210, s32[]{:T(128)S(6)} %select_n.37), kind=kOutput, calls=%fused_computation.3.clone.1 | convolution fusion | flops 3229614080 | bytes 25954308 | tf_op jit(solution)/shard_map/while/body/eval_jaxpr/dot_general | solution.py:89
  125.2 2.0 convert_reduce_fusion.2
  127.2 0.1 dynamic_slice.21
  127.3 9.4 %select_add_fusion.4 = f32[4096,768]{1,0:T(8,128)} fusion(f32[4096,768]{1,0:T(8,128)} %get-tuple-element.198, pred[]{:T(512)S(6)} %compare.6, s32[512]{0:T(512)S(1)} %dynamic_slice.21, bf16[2048,768]{1,0:T(8,128)(2,1)S(1)} %get-tuple-element.210, s32[]{:T(128)S(6)} %select_n.37), kind=kOutput, calls=%fused_computation.3.clone.1 | convolution fusion | flops 3229614080 | bytes 25954308 | tf_op jit(solution)/shard_map/while/body/eval_jaxpr/dot_general | solution.py:89
  136.7 2.0 convert_reduce_fusion.2
  138.7 0.1 dynamic_slice.21
  138.8 9.4 %select_add_fusion.4 = f32[4096,768]{1,0:T(8,128)} fusion(f32[4096,768]{1,0:T(8,128)} %get-tuple-element.198, pred[]{:T(512)S(6)} %compare.6, s32[512]{0:T(512)S(1)} %dynamic_slice.21, bf16[2048,768]{1,0:T(8,128)(2,1)S(1)} %get-tuple-element.210, s32[]{:T(128)S(6)} %select_n.37), kind=kOutput, calls=%fused_computation.3.clone.1 | convolution fusion | flops 3229614080 | bytes 25954308 | tf_op jit(solution)/shard_map/while/body/eval_jaxpr/dot_general | solution.py:89
  148.1 2.0 convert_reduce_fusion.2
  150.2 2.1 fusion.85
  152.2 2.7 collective-permute-start.1
  154.9 2.0 collective-permute-start
  156.9 29.6 %collective-permute-done.1 = f32[8,64,768]{2,1,0:T(8,128)S(1)} collective-permute-done((f32[8,64,768]{2,1,0:T(8,128)S(1)}, f32[8,64,768]{2,1,0:T(8,128)S(1)}, u32[]{:S(2)}, u32[]{:S(2)}) %collective-permute-start.1) | collective-permute-done | bytes 1572896 | tf_op jit(solution)/shard_map/ppermute | solution.py:19
  186.6 5.5 %collective-permute-done = f32[8,64,768]{2,1,0:T(8,128)S(1)} collective-permute-done((f32[8,64,768]{2,1,0:T(8,128)S(1)}, f32[8,64,768]{2,1,0:T(8,128)S(1)}, u32[]{:S(2)}, u32[]{:S(2)}) %collective-permute-start) | collective-permute-done | bytes 1572896 | tf_op jit(solution)/shard_map/ppermute | solution.py:18
  192.1 4.1 pad_maximum_fusion.3
  196.2 1.9 collective-permute-start.3
  198.1 4.1 collective-permute-start.2
  202.2 0.1 slice.313
  202.3 1.9 collective-permute-start.4
  204.2 0.1 reshape.70
  204.3 0.1 slice.315
  204.3 4.5 %collective-permute-start.5 = (f32[8,64]{1,0:T(8,128)S(1)}, f32[8,64]{1,0:T(8,128)S(1)}, u32[]{:S(2)}, u32[]{:S(2)}) collective-permute-start(f32[8,64]{1,0:T(8,128)S(1)} %slice.315), channel_id=1, source_target_pairs={{4,0},{8,4},{12,8},{16,12},{20,16},{24,20},{28,24},{5,1},{9,5},{13... | collective-permute-start | bytes 6152 | tf_op jit(solution)/shard_map/ppermute | solution.py:19
  208.9 0.0 collective-permute-done.4
  208.9 1.3 collective-permute-done.5
  210.2 0.1 fusion.86
  210.3 3.2 collective-permute-start.7
  213.4 2.7 collective-permute-start.6
  216.1 25.5 %collective-permute-done.7 = f32[80,8]{1,0:T(8,128)S(1)} collective-permute-done((f32[80,8]{1,0:T(8,128)S(1)}, f32[80,8]{1,0:T(8,128)S(1)}, u32[]{:S(2)}, u32[]{:S(2)}) %collective-permute-start.7) | collective-permute-done | bytes 2592 | tf_op jit(solution)/shard_map/ppermute | solution.py:19
  241.6 3.7 collective-permute-done.6
  245.3 0.1 pad_maximum_fusion.4
  245.4 0.1 fusion.64
  245.5 0.2 fusion.49
  245.7 0.0 collective-permute-done.3
  245.7 0.0 collective-permute-done.2
  245.7 13.4 %pad_maximum_fusion = f32[80,80,768]{2,1,0:T(8,128)} fusion(f32[80,8,768]{2,1,0:T(8,128)} %collective-permute-done.3, f32[8,64,768]{2,1,0:T(8,128)S(1)} %collective-permute-done.1, f32[64,64,768]{2,1,0:T(8,128)} %bitcast.32, f32[8,64,768]{2,1,0:T(8,128)S(1)} %collective-permute-done, f32[80,8,768]{2,1,0:T(8,128)} %collective-permute-done.2), kind=kLoop, calls=%fused_computation.12 | loop fusion | flops 19660800 | bytes 39321600 | tf_op jit(solution)/shard_map/concatenate | solution.py:20
  259.1 98.1 %fusion.7 = f32[64,80,768]{2,1,0:T(8,128)} fusion(f32[80,80,768]{2,1,0:T(8,128)} %pad_maximum_fusion), kind=kLoop, calls=%fused_computation.14 | loop fusion | flops 125829120 | bytes 283115520 | tf_op jit(solution)/shard_map/add | solution.py:30
  357.1 92.0 %fusion.39 = bf16[64,64,768]{2,1,0:T(8,128)(2,1)} fusion(bf16[64,64,768]{2,1,0:T(8,128)(2,1)} %param.9, f32[64,80,768]{2,1,0:T(8,128)} %fusion.7, f32[64,64]{1,0:T(8,128)S(1)} %fusion.49), kind=kLoop, calls=%fused_computation.79 | loop fusion | flops 116391936 | bytes 226508800 | tf_op jit(solution)/shard_map/convert_element_type | solution.py:111
  (17 shorter events, 0.1 us)
Async XLA Ops:
  16.8 13.9 %all-to-all-start = ((bf16[32,64,2]{1,2,0:T(2,128)(2,1)}), bf16[32,64,2]{1,2,0:T(2,128)(2,1)S(1)}, u32[]{:S(2)}, u32[]{:S(2)}) async-start(bf16[32,64,2]{1,2,0:T(2,128)(2,1)} %copy.23), calls=%async_computation | async-start | bytes 32768 | tf_op jit(solution)/shard_map/all_to_all | solution.py:67
  30.7 76.4 %all-to-all-start.1 = ((bf16[32,64,768]{2,1,0:T(8,128)(2,1)}), bf16[32,64,768]{2,1,0:T(8,128)(2,1)S(1)}, u32[]{:S(2)}, u32[]{:S(2)}) async-start(bf16[32,64,768]{2,1,0:T(8,128)(2,1)} %bitcast.34), calls=%async_computation.1 | async-start | bytes 6291456 | tf_op jit(solution)/shard_map/all_to_all | solution.py:60
  152.2 34.3 %collective-permute-start.1 = (f32[8,64,768]{2,1,0:T(8,128)S(1)}, f32[8,64,768]{2,1,0:T(8,128)S(1)}, u32[]{:S(2)}, u32[]{:S(2)}) collective-permute-start(f32[8,64,768]{2,1,0:T(8,128)S(1)} %bitcast.37), channel_id=1, source_target_pairs={{4,0},{8,4},{12,8},{16,12},{20,16},{24,20},{28,24},{5,1},{9,5},{13... | collective-permute-start | bytes 4718600 | tf_op jit(solution)/shard_map/ppermute | solution.py:19
  154.9 37.1 %collective-permute-start = (f32[8,64,768]{2,1,0:T(8,128)S(1)}, f32[8,64,768]{2,1,0:T(8,128)S(1)}, u32[]{:S(2)}, u32[]{:S(2)}) collective-permute-start(f32[8,64,768]{2,1,0:T(8,128)S(1)} %bitcast.36), channel_id=1, source_target_pairs={{0,4},{4,8},{8,12},{12,16},{16,20},{20,24},{24,28},{1,5},{5,9},{9,... | collective-permute-start | bytes 4718600 | tf_op jit(solution)/shard_map/ppermute | solution.py:18
  196.2 49.5 %collective-permute-start.3 = (f32[80,8,768]{2,1,0:T(8,128)}, f32[80,8,768]{2,1,0:T(8,128)}, u32[]{:S(2)}, u32[]{:S(2)}) collective-permute-start(f32[80,8,768]{2,1,0:T(8,128)} %get-tuple-element.148), channel_id=1, source_target_pairs={{1,0},{2,1},{3,2},{5,4},{6,5},{7,6},{9,8},{10,9},{11,10},{13,12},{... | collective-permute-start | bytes 5898248 | tf_op jit(solution)/shard_map/ppermute | solution.py:19
  198.1 47.6 %collective-permute-start.2 = (f32[80,8,768]{2,1,0:T(8,128)}, f32[80,8,768]{2,1,0:T(8,128)}, u32[]{:S(2)}, u32[]{:S(2)}) collective-permute-start(f32[80,8,768]{2,1,0:T(8,128)} %get-tuple-element.147), channel_id=1, source_target_pairs={{0,1},{1,2},{2,3},{4,5},{5,6},{6,7},{8,9},{9,10},{10,11},{12,13},{... | collective-permute-start | bytes 5898248 | tf_op jit(solution)/shard_map/ppermute | solution.py:18
  202.3 6.6 %collective-permute-start.4 = (f32[8,64]{1,0:T(8,128)S(1)}, f32[8,64]{1,0:T(8,128)S(1)}, u32[]{:S(2)}, u32[]{:S(2)}) collective-permute-start(f32[8,64]{1,0:T(8,128)S(1)} %slice.313), channel_id=1, source_target_pairs={{0,4},{4,8},{8,12},{12,16},{16,20},{20,24},{24,28},{1,5},{5,9},{9,... | collective-permute-start | bytes 6152 | tf_op jit(solution)/shard_map/ppermute | solution.py:18
  204.3 5.8 %collective-permute-start.5 = (f32[8,64]{1,0:T(8,128)S(1)}, f32[8,64]{1,0:T(8,128)S(1)}, u32[]{:S(2)}, u32[]{:S(2)}) collective-permute-start(f32[8,64]{1,0:T(8,128)S(1)} %slice.315), channel_id=1, source_target_pairs={{4,0},{8,4},{12,8},{16,12},{20,16},{24,20},{28,24},{5,1},{9,5},{13... | collective-permute-start | bytes 6152 | tf_op jit(solution)/shard_map/ppermute | solution.py:19
  210.3 31.3 %collective-permute-start.7 = (f32[80,8]{1,0:T(8,128)S(1)}, f32[80,8]{1,0:T(8,128)S(1)}, u32[]{:S(2)}, u32[]{:S(2)}) collective-permute-start(f32[80,8]{1,0:T(8,128)S(1)} %get-tuple-element.152), channel_id=1, source_target_pairs={{1,0},{2,1},{3,2},{5,4},{6,5},{7,6},{9,8},{10,9},{11,10},{13,12},{... | collective-permute-start | bytes 7688 | tf_op jit(solution)/shard_map/ppermute | solution.py:19
  213.4 31.9 %collective-permute-start.6 = (f32[80,8]{1,0:T(8,128)S(1)}, f32[80,8]{1,0:T(8,128)S(1)}, u32[]{:S(2)}, u32[]{:S(2)}) collective-permute-start(f32[80,8]{1,0:T(8,128)S(1)} %get-tuple-element.151), channel_id=1, source_target_pairs={{0,1},{1,2},{2,3},{4,5},{5,6},{6,7},{8,9},{9,10},{10,11},{12,13},{... | collective-permute-start | bytes 7688 | tf_op jit(solution)/shard_map/ppermute | solution.py:18
where the time goes:
time: 450 us; the launch traced here: 449 us
  other arithmetic  228 us (51%)
  waiting for transfers between devices  136 us (30%)
  starting transfers between devices  34.8 us (8%)
  matrix products  34.7 us (8%)
  local copies, waits for them, and re-layouts  15.4 us (3%)
    add x2, other arithmetic, smooth_along(): result + weights[place] * lax.slice_in_dim(values_in, place, place + exte...  98.1 us
    convert_element_type x1, other arithmetic, on_device(): return updated.astype(jnp.bfloat16)  92 us
    all_to_all x1, waiting for transfers between devices, on_device(): lax.all_to_all(outgoing.reshape(tile_total, capacity, feature), ('mx', 'm...  70.4 us
    ppermute x4, waiting for transfers between devices, extended(): after = lax.ppermute(leading, axis, down)  56.4 us
    dot_general x4, matrix products, accumulate(): lax.dot_general(one_hot, block_docs, (((0,), (0,)), ((), ())), preferred_...  34.7 us
    concatenate x2, other arithmetic, extended(): x = jnp.concatenate([before, x, after], axis=dim)  13.5 us
    ppermute x4, starting transfers between devices, extended(): after = lax.ppermute(leading, axis, down)  12.3 us
    ppermute x4, starting transfers between devices, extended(): before = lax.ppermute(last, axis, up)  10.7 us
  transfers between devices with their start and end apart: 10, of which 6 were waited for; matrix products, arithmetic and copies ran while one was open for 2% of the time, Pallas kernels for 0%

commit v1 on v0

v1 whole, which is shorter than its diff:
```python
import functools
import math

import jax
import jax.numpy as jnp
import numpy as np
from jax import lax
from jax.experimental import pallas as pl
from jax.experimental.pallas import tpu as pltpu
from jax.sharding import PartitionSpec as P

RADIUS = 8
CHUNKS = 3
WEIGHTS = [math.exp(-2.0 * k * k / RADIUS**2) for k in range(-RADIUS, RADIUS + 1)]
AXES = ("mx", "my")


def pack_kernel(tiles, cap, cols, block, own_ref, unit_ref, docs_ref, marks_ref, *rest):
    outs, place_ref = rest[:-1], rest[-1]
    count = docs_ref.shape[0]
    step = pl.program_id(0)

    @pl.when(step == 0)
    def _():
        own = own_ref[...]
        tile = lax.broadcasted_iota(jnp.int32, (tiles, count), 0)
        mine = jnp.where(tile == own, 1.0, 0.0)
        before = lax.broadcasted_iota(jnp.int32, (count, count), 0)
        after = lax.broadcasted_iota(jnp.int32, (count, count), 1)
        tri = jnp.where(before < after, 1.0, 0.0).astype(jnp.bfloat16)
        earlier = jnp.dot(mine.astype(jnp.bfloat16), tri, preferred_element_type=jnp.float32)
        slot = jnp.sum(mine * earlier, axis=0, keepdims=True)
        place_ref[...] = own * cap + slot.astype(jnp.int32)

    here = lax.broadcasted_iota(jnp.int32, (block, count), 0) + step * block
    pick = jnp.where(here == place_ref[...], 1.0, 0.0).astype(jnp.bfloat16)
    unit = unit_ref[...]
    line = lax.broadcasted_iota(jnp.int32, (16, count), 0)
    mark = jnp.where(line == 0, unit // cols + 1, jnp.where(line == 1, unit % cols + 1, 0))
    marks_ref[...] = lax.dot_general(
        mark.astype(jnp.float32).astype(jnp.bfloat16),
        pick,
        (((1,), (1,)), ((), ())),
        preferred_element_type=jnp.float32,
    ).astype(jnp.bfloat16)
    width = outs[0].shape[1]
    for k, out in enumerate(outs):
        out[...] = jnp.dot(
            pick, docs_ref[:, k * width : (k + 1) * width], preferred_element_type=jnp.float32
        ).astype(jnp.bfloat16)


def pack(own, unit, docs, tiles, cap, cols):
    count, feature = docs.shape
    slots, width = tiles * cap, feature // CHUNKS
    block = 256
    return pl.pallas_call(
        functools.partial(pack_kernel, tiles, cap, cols, block),
        grid=(slots // block,),
        in_specs=[
            pl.BlockSpec((1, count), lambda i: (0, 0)),
            pl.BlockSpec((1, count), lambda i: (0, 0)),
            pl.BlockSpec((count, feature), lambda i: (0, 0)),
        ],
        out_specs=[pl.BlockSpec((16, block), lambda i: (0, i))]
        + [pl.BlockSpec((block, width), lambda i: (i, 0))] * CHUNKS,
        out_shape=[jax.ShapeDtypeStruct((16, slots), jnp.bfloat16)]
        + [jax.ShapeDtypeStruct((slots, width), jnp.bfloat16)] * CHUNKS,
        scratch_shapes=[pltpu.VMEM((1, count), jnp.int32)],
        compiler_params=pltpu.CompilerParams(vmem_limit_bytes=40 << 20),
        cost_estimate=pl.CostEstimate(
            flops=2 * slots * count * feature, bytes_accessed=6 << 20, transcendentals=0
        ),
        name="pack",
    )(own, unit, docs)


def gather_kernel(block, ids_ref, docs_ref, num_ref):
    here = lax.broadcasted_iota(jnp.int32, (block, ids_ref.shape[1]), 0)
    hot = jnp.where(here == ids_ref[...] - pl.program_id(0) * block, 1.0, 0.0)
    num_ref[...] = jnp.dot(
        hot.astype(jnp.bfloat16), docs_ref[...], preferred_element_type=jnp.float32
    )


def accumulate(ids, docs, units):
    slots, width = docs.shape
    block = min(512, units)
    return pl.pallas_call(
        functools.partial(gather_kernel, block),
        grid=(units // block,),
        in_specs=[
            pl.BlockSpec((1, slots), lambda i: (0, 0)),
            pl.BlockSpec((slots, width), lambda i: (0, 0)),
        ],
        out_specs=pl.BlockSpec((block, width), lambda i: (i, 0)),
        out_shape=jax.ShapeDtypeStruct((units, width), jnp.float32),
        compiler_params=pltpu.CompilerParams(vmem_limit_bytes=40 << 20),
        cost_estimate=pl.CostEstimate(
            flops=2 * units * slots * width, bytes_accessed=5 << 20, transcendentals=0
        ),
        name="accumulate",
    )(ids, docs)


def smooth_kernel(
    num_ref, top_ref, bot_ref, left_ref, right_ref, band_ref, inv_ref, code_ref, *rest
):
    out_ref, ext, split = rest[-3:]
    rows, cols, width = num_ref.shape
    tall, wide = rows + 2 * RADIUS, cols + 2 * RADIUS
    ext[0:RADIUS, RADIUS : RADIUS + cols, :] = top_ref[...].astype(jnp.float32)
    ext[RADIUS : RADIUS + rows, RADIUS : RADIUS + cols, :] = num_ref[...]
    ext[RADIUS + rows :, RADIUS : RADIUS + cols, :] = bot_ref[...].astype(jnp.float32)
    ext[:, 0:RADIUS, :] = left_ref[...].astype(jnp.float32)
    ext[:, RADIUS + cols :, :] = right_ref[...].astype(jnp.float32)
    group, lanes, high = 4, 128, 16

    def down(step, carry):
        base = step * group
        for c in range(0, wide, high):
            for f in range(0, width, lanes):
                x = [
                    ext[base + i, c : c + high, f : f + lanes] for i in range(group + 2 * RADIUS)
                ]
                for g in range(group):
                    total = x[g + RADIUS]
                    for k in range(RADIUS):
                        total = total + WEIGHTS[k] * (x[g + k] + x[g + 2 * RADIUS - k])
                    main = total.astype(jnp.bfloat16)
                    small = (total - main.astype(jnp.float32)).astype(jnp.bfloat16)
                    split[base + g, c : c + high, f : f + lanes] = main
                    split[base + g, wide + c : wide + c + high, f : f + lanes] = small
                    split[base + g, 2 * wide + c : 2 * wide + c + high, f : f + lanes] = main
        return carry

    lax.fori_loop(0, rows // group, down, 0)

    def across(step, carry):
        for g in range(2):
            r = step * 2 + g
            y = jnp.dot(band_ref[...], split[r], preferred_element_type=jnp.float32)
            inv = inv_ref[r]
            for f in range(0, width, lanes):
                code = code_ref[r, :, f : f + lanes].astype(jnp.float32)
                out_ref[r, :, f : f + lanes] = (
                    (y[:, f : f + lanes] + 8.0 * code) * inv
                ).astype(jnp.bfloat16)
        return carry

    lax.fori_loop(0, rows // 2, across, 0)


def smooth(part, num, top, bot, left, right, band, inv, codebook, result):
    rows, cols, width = num.shape
    feature = codebook.shape[2]
    block = 256 if width % 256 == 0 else width
    first = part * (width // block)
    tall, wide = rows + 2 * RADIUS, cols + 2 * RADIUS

    def spec(a, b, offset=0):
        return pl.BlockSpec((a, b, block), lambda i: (0, 0, i + offset))

    held = [] if result is None else [result]
    return pl.pallas_call(
        smooth_kernel,
        grid=(width // block,),
        in_specs=[
            spec(rows, cols),
            spec(RADIUS, cols),
            spec(RADIUS, cols),
            spec(tall, RADIUS),
            spec(tall, RADIUS),
            pl.BlockSpec(band.shape, lambda i: (0, 0)),
            pl.BlockSpec(inv.shape, lambda i: (0, 0, 0)),
            spec(rows, cols, first),
        ]
        + [pl.BlockSpec(memory_space=pl.ANY)] * len(held),
        out_specs=spec(rows, cols, first),
        out_shape=jax.ShapeDtypeStruct((rows, cols, feature), jnp.bfloat16),
        input_output_aliases={8: 0} if held else {},
        scratch_shapes=[
            pltpu.VMEM((tall, wide, block), jnp.float32),
            pltpu.VMEM((rows, 3 * wide, block), jnp.bfloat16),
        ],
        compiler_params=pltpu.CompilerParams(vmem_limit_bytes=56 << 20),
        cost_estimate=pl.CostEstimate(
            flops=12 * 10**9 // CHUNKS, bytes_accessed=30 * 2**20 // CHUNKS, transcendentals=0
        ),
        name="smooth",
    )(num, top, bot, left, right, band, inv, codebook, *held)


def shifts(axis):
    n = lax.axis_size(axis)
    up = [(i, i + 1) for i in range(n - 1)]
    return up, [(j, i) for i, j in up]


def halo(x, dtype):
    rows, cols = x.shape[:2]
    up, down = shifts("mx")
    top = lax.ppermute(x[rows - RADIUS :].astype(dtype), "mx", up)
    bot = lax.ppermute(x[:RADIUS].astype(dtype), "mx", down)
    up, down = shifts("my")

    def side(a, b):
        return jnp.concatenate([top[:, a:b], x[:, a:b].astype(dtype), bot[:, a:b]], axis=0)

    left = lax.ppermute(side(cols - RADIUS, cols), "my", up)
    right = lax.ppermute(side(0, RADIUS), "my", down)
    return top, bot, left, right


def banded(extent):
    full = np.zeros((extent, extent + 2 * RADIUS), np.float32)
    for r in range(extent):
        full[r, r : r + 2 * RADIUS + 1] = WEIGHTS
    return full


def on_device(documents, owner_tile, unit_in_tile, codebook):
    tiles = lax.axis_size("mx") * lax.axis_size("my")
    rows, cols, feature = codebook.shape
    count = documents.shape[0]
    cap = max(2, 2 * count // tiles)
    marks, *sent = pack(
        owner_tile.reshape(1, count), unit_in_tile.reshape(1, count), documents, tiles, cap, cols
    )

    def exchange(x, axis):
        return lax.all_to_all(x, AXES, split_axis=axis, concat_axis=axis, tiled=True)

    marks = exchange(marks[:2].reshape(2, tiles, cap), 1).reshape(2, tiles * cap)
    got = [exchange(x.reshape(tiles, cap, -1), 0).reshape(tiles * cap, -1) for x in sent]
    spot = marks.astype(jnp.int32) - 1
    ids = jnp.where(spot[0] < 0, -1, spot[0] * cols + spot[1])[None, :]
    in_row = (spot[0][None, :] == jnp.arange(rows)[:, None]).astype(jnp.bfloat16)
    in_col = (spot[1][None, :] == jnp.arange(cols)[:, None]).astype(jnp.bfloat16)
    hits = lax.dot_general(
        in_row, in_col, (((1,), (1,)), ((), ())), preferred_element_type=jnp.float32
    )
    top, bot, left, right = halo(hits, jnp.float32)
    hits = jnp.concatenate([left, jnp.concatenate([top, hits, bot], 0), right], 1)
    exact = lax.Precision.HIGHEST
    hits = jnp.dot(
        jnp.dot(jnp.asarray(banded(rows)), hits, precision=exact),
        jnp.asarray(banded(cols).T),
        precision=exact,
    )
    inv = jnp.broadcast_to((1.0 / (hits + 8.0))[:, :, None], (rows, cols, 128))
    full = banded(cols)
    main = full.astype(jnp.bfloat16)
    small = (full - main.astype(np.float32)).astype(jnp.bfloat16)
    band = jnp.asarray(np.concatenate([main, main, small], axis=1))

    result = None
    for part, docs in enumerate(got):
        num = accumulate(ids, docs, rows * cols).reshape(rows, cols, -1)
        result = smooth(part, num, *halo(num, jnp.bfloat16), band, inv, codebook, result)
    return result


def solution(mesh):
    return jax.shard_map(
        on_device,
        mesh=mesh,
        in_specs=(P(AXES, None), P(AXES, None), P(AXES), P("mx", "my", None)),
        out_specs=P("mx", "my", None),
        check_vma=False,
    )
```

time: 450 us -> 201 us (0.45)
  other arithmetic: 228 us -> 2.11 us
  waiting for transfers between devices: 136 us -> 12.3 us
  Pallas kernels: 0 us -> 72.3 us
  blocking collectives: 0 us -> 40.1 us
  matrix products: 34.7 us -> 0.75 us
  starting transfers between devices: 34.8 us -> 57.3 us
    add x8 -> x0, other arithmetic: 98.4 us -> none  [the longest x2 98.1 us: smooth_along(): result + weights[place] * lax.slice_in_dim(values_in, place, place + exte...]
    convert_element_type x2 -> x0, other arithmetic: 92.7 us -> none  [the longest x1 92 us: on_device(): return updated.astype(jnp.bfloat16)]
    pallas_call x0 -> x7, Pallas kernels: none -> 72.3 us  [the longest x3 48.3 us: smooth(): pl.pallas_call(smooth_kernel, grid=(width // block,), in_specs=[spec(rows...]
    ppermute x8 -> x16, waiting for transfers between devices: 65.6 us -> 1.95 us  [the longest x4 1.92 us: halo(): top = lax.ppermute(x[rows - RADIUS:].astype(dtype), 'mx', up)]
    all_to_all x2, waiting for transfers between devices: 70.4 us -> 10.3 us  [exchange(): lax.all_to_all(x, AXES, split_axis=axis, concat_axis=axis, tiled=True)]
    all_to_all x0 -> x2, blocking collectives: none -> 40.1 us  [exchange(): lax.all_to_all(x, AXES, split_axis=axis, concat_axis=axis, tiled=True)]
    dot_general x4 -> x3, matrix products: 34.7 us -> 0.75 us  [the longest x1 0.26 us: on_device(): lax.dot_general(in_row, in_col, (((1,), (1,)), ((), ())), preferred_eleme...]
    ppermute x8 -> x16, starting transfers between devices: 23 us -> 49.2 us  [the longest x4 17.9 us: halo(): bot = lax.ppermute(x[:RADIUS].astype(dtype), 'mx', down)]
  transfers between devices with their start and end apart: 10 -> 18, of which waited for: 6 -> 2; matrix products, arithmetic and copies ran while one was open for 2% -> 3% of each run, Pallas kernels for 0% -> 25%
where the time goes in v1:
time: 201 us
  Pallas kernels  72.3 us (36%)
  starting transfers between devices  57.3 us (29%)
  blocking collectives  40.1 us (20%)
  local copies, waits for them, and re-layouts  15.1 us (8%)
  waiting for transfers between devices  12.3 us (6%)
  other arithmetic  2.11 us (1%)
    pallas_call x3, Pallas kernels, smooth(): pl.pallas_call(smooth_kernel, grid=(width // block,), in_specs=[spec(rows...  48.3 us
    all_to_all x2, blocking collectives, exchange(): lax.all_to_all(x, AXES, split_axis=axis, concat_axis=axis, tiled=True)  40.1 us
    ppermute x4, starting transfers between devices, halo(): bot = lax.ppermute(x[:RADIUS].astype(dtype), 'mx', down)  17.9 us
    pallas_call x3, Pallas kernels, accumulate(): pl.pallas_call(functools.partial(gather_kernel, block), grid=(units // bl...  17.2 us
    ppermute x4, starting transfers between devices, halo(): left = lax.ppermute(side(cols - RADIUS, cols), 'my', up)  13.3 us
    unnamed x40, local copies, waits for them, and re-layouts  11 us
    all_to_all x2, waiting for transfers between devices, exchange(): lax.all_to_all(x, AXES, split_axis=axis, concat_axis=axis, tiled=True)  10.3 us
    ppermute x4, starting transfers between devices, halo(): right = lax.ppermute(side(0, RADIUS), 'my', down)  10 us
  transfers between devices with their start and end apart: 18, of which 2 were waited for; matrix products, arithmetic and copies ran while one was open for 3% of the time, Pallas kernels for 25%

profile of v1, /device:TPU:12, one launch (start us, length us, event | category | flops | bytes accessed | tf_op | source)
XLA Modules:
  0.0 200.6 jit_solution(15553813588821934023)
XLA Ops:
  0.0 1.4 copy-done.3
  1.4 0.7 copy-done.4
  2.1 0.7 copy-done.5
  2.8 6.9 %pack.1 = (bf16[16,2048]{1,0:T(8,128)(2,1)S(1)}, bf16[2048,256]{1,0:T(8,128)(2,1)}, bf16[2048,256]{1,0:T(8,128)(2,1)S(1)}, bf16[2048,256]{1,0:T(8,128)(2,1)}) custom-call(s32[1,1024]{1,0:T(1,128)S(1)} %bitcast.30, s32[1,1024]{1,0:T(1,128)S(1)} %bitcast.31, bf16[1024,768]{1,0:T(8,128)(2,1)S(1)} %copy-done.3), custom_call_target="tpu_custom_call" | custom-call | flops 3221225472 | bytes 6291456 | tf_op jit(solution)/shard_map/pack/pallas_call | solution.py:57
  9.7 0.1 reshape.64
  9.8 10.8 %all_to_all.20 = bf16[2,32,64]{2,0,1:T(2,128)(2,1)S(1)} all-to-all(bf16[2,32,64]{2,0,1:T(2,128)(2,1)S(1)} %copy.10), channel_id=1, replica_groups=mesh['mx'=8,'my'=4] {'mx','my'}, dimensions={1} | all-to-all | bytes 16384 | tf_op jit(solution)/shard_map/all_to_all | solution.py:232
  20.6 29.3 %all_to_all.21 = bf16[32,64,256]{2,1,0:T(8,128)(2,1)S(1)} all-to-all(bf16[32,64,256]{2,1,0:T(8,128)(2,1)S(1)} %bitcast.29), channel_id=1, replica_groups=mesh['mx'=8,'my'=4] {'mx','my'}, dimensions={0} | all-to-all | bytes 2097152 | tf_op jit(solution)/shard_map/all_to_all | solution.py:232
  49.9 4.0 %all-to-all-start.3 = ((bf16[32,64,256]{2,1,0:T(8,128)(2,1)}), bf16[32,64,256]{2,1,0:T(8,128)(2,1)S(1)}, u32[]{:S(2)}, u32[]{:S(2)}) async-start(bf16[32,64,256]{2,1,0:T(8,128)(2,1)} %bitcast.12), calls=%async_computation.3 | async-start | bytes 2097152 | tf_op jit(solution)/shard_map/all_to_all | solution.py:232
  53.9 0.1 slice_reduce_fusion.1
  54.1 0.1 eq.30
  54.2 0.1 eq.34
  54.2 0.3 fusion.1
  54.5 0.1 fusion.31
  54.6 2.1 %collective-permute-start.4 = (f32[8,64]{0,1:T(8,128)S(1)}, f32[8,64]{0,1:T(8,128)S(1)}, u32[]{:S(2)}, u32[]{:S(2)}) collective-permute-start(f32[8,64]{0,1:T(8,128)S(1)} %get-tuple-element.46), channel_id=1, source_target_pairs={{0,4},{4,8},{8,12},{12,16},{16,20},{20,24},{24,28},{1,5},{5,9},{9,... | collective-permute-start | bytes 6152 | tf_op jit(solution)/shard_map/ppermute | solution.py:203
  56.7 4.4 %collective-permute-start.5 = (f32[8,64]{0,1:T(8,128)S(1)}, f32[8,64]{0,1:T(8,128)S(1)}, u32[]{:S(2)}, u32[]{:S(2)}) collective-permute-start(f32[8,64]{0,1:T(8,128)S(1)} %get-tuple-element.47), channel_id=1, source_target_pairs={{4,0},{8,4},{12,8},{16,12},{20,16},{24,20},{28,24},{5,1},{9,5},{13... | collective-permute-start | bytes 6152 | tf_op jit(solution)/shard_map/ppermute | solution.py:204
  61.1 1.9 collective-permute-done.4
  63.0 0.1 pad_maximum_fusion.6
  63.1 3.2 %collective-permute-start.6 = (f32[80,8]{0,1:T(8,128)S(1)}, f32[80,8]{0,1:T(8,128)S(1)}, u32[]{:S(2)}, u32[]{:S(2)}) collective-permute-start(f32[80,8]{0,1:T(8,128)S(1)} %pad_maximum_fusion.6), channel_id=1, source_target_pairs={{0,1},{1,2},{2,3},{4,5},{5,6},{6,7},{8,9},{9,10},{10,11},{12,13},{... | collective-permute-start | bytes 7688 | tf_op jit(solution)/shard_map/ppermute | solution.py:210
  66.3 0.1 pad_maximum_fusion.7
  66.4 2.6 %collective-permute-start.7 = (f32[80,8]{0,1:T(8,128)S(1)}, f32[80,8]{0,1:T(8,128)S(1)}, u32[]{:S(2)}, u32[]{:S(2)}) collective-permute-start(f32[80,8]{0,1:T(8,128)S(1)} %pad_maximum_fusion.7), channel_id=1, source_target_pairs={{1,0},{2,1},{3,2},{5,4},{6,5},{7,6},{9,8},{10,9},{11,10},{13,12},{... | collective-permute-start | bytes 7688 | tf_op jit(solution)/shard_map/ppermute | solution.py:211
  69.0 0.1 reshape.75.ids_ref
  69.1 10.3 %all-to-all-done.3 = bf16[32,64,256]{2,1,0:T(8,128)(2,1)S(1)} async-done(((bf16[32,64,256]{2,1,0:T(8,128)(2,1)}), bf16[32,64,256]{2,1,0:T(8,128)(2,1)S(1)}, u32[]{:S(2)}, u32[]{:S(2)}) %all-to-all-start.3) | async-done | bytes 1048608 | tf_op jit(solution)/shard_map/all_to_all | solution.py:232
  79.4 4.1 %all-to-all-start.1 = ((bf16[32,64,256]{2,1,0:T(8,128)(2,1)}), bf16[32,64,256]{2,1,0:T(8,128)(2,1)S(1)}, u32[]{:S(2)}, u32[]{:S(2)}) async-start(bf16[32,64,256]{2,1,0:T(8,128)(2,1)} %bitcast.2), calls=%async_computation.1 | async-start | bytes 2097152 | tf_op jit(solution)/shard_map/all_to_all | solution.py:232
  83.5 0.0 collective-permute-done.7
  83.5 0.2 fusion.4
  83.8 0.2 fusion
  84.0 5.7 %accumulate.5 = f32[4096,256]{1,0:T(8,128)S(1)} custom-call(s32[1,2048]{1,0:T(1,128)S(1)} %reshape.75.ids_ref, bf16[2048,256]{1,0:T(8,128)(2,1)S(1)} %bitcast.27), custom_call_target="tpu_custom_call" | custom-call | flops 4294967296 | bytes 5242880 | tf_op jit(solution)/shard_map/accumulate/pallas_call | solution.py:89
  89.8 0.2 convert.28
  90.0 1.8 copy-done
  91.8 0.3 convert.29
  92.1 0.8 fusion.17
  92.9 2.0 %collective-permute-start.12 = (bf16[8,64,256]{2,1,0:T(8,128)(2,1)}, bf16[8,64,256]{2,1,0:T(8,128)(2,1)S(1)}, u32[]{:S(2)}, u32[]{:S(2)}) collective-permute-start(bf16[8,64,256]{2,1,0:T(8,128)(2,1)} %bitcast.15), channel_id=1, source_target_pairs={{0,4},{4,8},{8,12},{12,16},{16,20},{20,24},{24,28},{1,5},{5,9},{9,... | collective-permute-start | bytes 786440 | tf_op jit(solution)/shard_map/ppermute | solution.py:203
  95.0 4.4 %collective-permute-start.13 = (bf16[8,64,256]{2,1,0:T(8,128)(2,1)}, bf16[8,64,256]{2,1,0:T(8,128)(2,1)S(1)}, u32[]{:S(2)}, u32[]{:S(2)}) collective-permute-start(bf16[8,64,256]{2,1,0:T(8,128)(2,1)} %bitcast.16), channel_id=1, source_target_pairs={{4,0},{8,4},{12,8},{16,12},{20,16},{24,20},{28,24},{5,1},{9,5},{13... | collective-permute-start | bytes 786440 | tf_op jit(solution)/shard_map/ppermute | solution.py:204
  99.4 5.7 %accumulate.4 = f32[4096,256]{1,0:T(8,128)S(1)} custom-call(s32[1,2048]{1,0:T(1,128)S(1)} %reshape.75.ids_ref, bf16[2048,256]{1,0:T(8,128)(2,1)S(1)} %bitcast.26), custom_call_target="tpu_custom_call" | custom-call | flops 4294967296 | bytes 5242880 | tf_op jit(solution)/shard_map/accumulate/pallas_call | solution.py:89
  105.2 0.2 convert.26
  105.4 1.8 copy-done.1
  107.2 0.3 convert.27
  107.5 0.7 fusion.19
  108.2 1.9 collective-permute-start.8
  110.1 4.5 %collective-permute-start.9 = (bf16[8,64,256]{2,1,0:T(8,128)(2,1)S(1)}, bf16[8,64,256]{2,1,0:T(8,128)(2,1)S(1)}, u32[]{:S(2)}, u32[]{:S(2)}) collective-permute-start(bf16[8,64,256]{2,1,0:T(8,128)(2,1)S(1)} %bitcast.32), channel_id=1, source_target_pairs={{4,0},{8,4},{12,8},{16,12},{20,16},{24,20},{28,24},{5,1},{9,5},{13... | collective-permute-start | bytes 786440 | tf_op jit(solution)/shard_map/ppermute | solution.py:204
  114.8 0.0 all-to-all-done.1
  114.8 5.7 %accumulate.3 = f32[4096,256]{1,0:T(8,128)S(1)} custom-call(s32[1,2048]{1,0:T(1,128)S(1)} %reshape.75.ids_ref, bf16[2048,256]{1,0:T(8,128)(2,1)S(1)} %bitcast.28), custom_call_target="tpu_custom_call" | custom-call | flops 4294967296 | bytes 5242880 | tf_op jit(solution)/shard_map/accumulate/pallas_call | solution.py:89
  120.5 0.3 convert.25
  120.9 1.6 copy-done.2
  122.5 0.2 convert.24
  122.7 1.9 collective-permute-start
  124.6 0.0 collective-permute-done.12.top_ref
  124.7 4.5 %collective-permute-start.1 = (bf16[8,64,256]{2,1,0:T(8,128)(2,1)S(1)}, bf16[8,64,256]{2,1,0:T(8,128)(2,1)S(1)}, u32[]{:S(2)}, u32[]{:S(2)}) collective-permute-start(bf16[8,64,256]{2,1,0:T(8,128)(2,1)S(1)} %bitcast.33), channel_id=1, source_target_pairs={{4,0},{8,4},{12,8},{16,12},{20,16},{24,20},{28,24},{5,1},{9,5},{13... | collective-permute-start | bytes 786440 | tf_op jit(solution)/shard_map/ppermute | solution.py:204
  129.3 3.4 %collective-permute-start.14 = (bf16[80,8,256]{2,1,0:T(8,128)(2,1)S(1)}, bf16[80,8,256]{2,1,0:T(8,128)(2,1)S(1)}, u32[]{:S(2)}, u32[]{:S(2)}) collective-permute-start(bf16[80,8,256]{2,1,0:T(8,128)(2,1)S(1)} %pad_maximum_fusion.4), channel_id=1, source_target_pairs={{0,1},{1,2},{2,3},{4,5},{5,6},{6,7},{8,9},{9,10},{10,11},{12,13},{... | collective-permute-start | bytes 983048 | tf_op jit(solution)/shard_map/ppermute | solution.py:210
  132.8 2.5 %collective-permute-start.15 = (bf16[80,8,256]{2,1,0:T(8,128)(2,1)S(1)}, bf16[80,8,256]{2,1,0:T(8,128)(2,1)S(1)}, u32[]{:S(2)}, u32[]{:S(2)}) collective-permute-start(bf16[80,8,256]{2,1,0:T(8,128)(2,1)S(1)} %pad_maximum_fusion.5), channel_id=1, source_target_pairs={{1,0},{2,1},{3,2},{5,4},{6,5},{7,6},{9,8},{10,9},{11,10},{13,12},{... | collective-permute-start | bytes 983048 | tf_op jit(solution)/shard_map/ppermute | solution.py:211
  135.3 0.0 collective-permute-done.9.bot_ref
  135.4 3.4 %collective-permute-start.10 = (bf16[80,8,256]{2,1,0:T(8,128)(2,1)S(1)}, bf16[80,8,256]{2,1,0:T(8,128)(2,1)S(1)}, u32[]{:S(2)}, u32[]{:S(2)}) collective-permute-start(bf16[80,8,256]{2,1,0:T(8,128)(2,1)S(1)} %pad_maximum_fusion.2), channel_id=1, source_target_pairs={{0,1},{1,2},{2,3},{4,5},{5,6},{6,7},{8,9},{9,10},{10,11},{12,13},{... | collective-permute-start | bytes 983048 | tf_op jit(solution)/shard_map/ppermute | solution.py:210
  138.8 0.0 collective-permute-done.top_ref
  138.8 2.5 %collective-permute-start.11 = (bf16[80,8,256]{2,1,0:T(8,128)(2,1)S(1)}, bf16[80,8,256]{2,1,0:T(8,128)(2,1)S(1)}, u32[]{:S(2)}, u32[]{:S(2)}) collective-permute-start(bf16[80,8,256]{2,1,0:T(8,128)(2,1)S(1)} %pad_maximum_fusion.3), channel_id=1, source_target_pairs={{1,0},{2,1},{3,2},{5,4},{6,5},{7,6},{9,8},{10,9},{11,10},{13,12},{... | collective-permute-start | bytes 983048 | tf_op jit(solution)/shard_map/ppermute | solution.py:211
  141.4 3.4 %collective-permute-start.2 = (bf16[80,8,256]{2,1,0:T(8,128)(2,1)S(1)}, bf16[80,8,256]{2,1,0:T(8,128)(2,1)S(1)}, u32[]{:S(2)}, u32[]{:S(2)}) collective-permute-start(bf16[80,8,256]{2,1,0:T(8,128)(2,1)S(1)} %pad_maximum_fusion), channel_id=1, source_target_pairs={{0,1},{1,2},{2,3},{4,5},{5,6},{6,7},{8,9},{9,10},{10,11},{12,13},{... | collective-permute-start | bytes 983048 | tf_op jit(solution)/shard_map/ppermute | solution.py:210
  144.9 2.5 %collective-permute-start.3 = (bf16[80,8,256]{2,1,0:T(8,128)(2,1)S(1)}, bf16[80,8,256]{2,1,0:T(8,128)(2,1)S(1)}, u32[]{:S(2)}, u32[]{:S(2)}) collective-permute-start(bf16[80,8,256]{2,1,0:T(8,128)(2,1)S(1)} %pad_maximum_fusion.1), channel_id=1, source_target_pairs={{1,0},{2,1},{3,2},{5,4},{6,5},{7,6},{9,8},{10,9},{11,10},{13,12},{... | collective-permute-start | bytes 983048 | tf_op jit(solution)/shard_map/ppermute | solution.py:211
  147.4 1.9 broadcast_in_dim.7.inv_ref
  149.3 16.1 %smooth.3.rest_0_ = bf16[64,64,768]{2,1,0:T(8,128)(2,1)} custom-call(f32[64,64,256]{2,1,0:T(8,128)} %bitcast.21, bf16[8,64,256]{2,1,0:T(8,128)(2,1)} %copy-done.6, bf16[8,64,256]{2,1,0:T(8,128)(2,1)} %copy-done.8, bf16[80,8,256]{2,1,0:T(8,128)(2,1)} %copy-done.12, bf16[80,8,256]{2,1,0:T(8,128)(2,1)} %copy-done.13, bf16[64,240]{1,0:T(8,128)(2,1)} %constant.20.clone.band_ref, ...), custom_call_target="tpu_custom_call" | custom-call | flops 4000000000 | bytes 10485760 | tf_op jit(solution)/shard_map/smooth/pallas_call | solution.py:165
  165.5 0.7 copy-done.14
  166.2 0.7 copy-done.15
  166.9 16.1 %smooth.4.rest_0_ = bf16[64,64,768]{2,1,0:T(8,128)(2,1)} custom-call(f32[64,64,256]{2,1,0:T(8,128)} %bitcast.23, bf16[8,64,256]{2,1,0:T(8,128)(2,1)} %copy-done.7, bf16[8,64,256]{2,1,0:T(8,128)(2,1)} %copy-done.9, bf16[80,8,256]{2,1,0:T(8,128)(2,1)} %copy-done.14, bf16[80,8,256]{2,1,0:T(8,128)(2,1)} %copy-done.15, ...), custom_call_target="tpu_custom_call", output_to_operand_aliasing={{}: (8, {})} | custom-call | flops 4000000000 | bytes 10485760 | tf_op jit(solution)/shard_map/smooth/pallas_call | solution.py:165
  183.0 0.7 copy-done.16
  183.7 0.7 copy-done.17
  184.5 16.1 %smooth.5 = bf16[64,64,768]{2,1,0:T(8,128)(2,1)} custom-call(f32[64,64,256]{2,1,0:T(8,128)} %bitcast.25, bf16[8,64,256]{2,1,0:T(8,128)(2,1)} %copy-done.10, bf16[8,64,256]{2,1,0:T(8,128)(2,1)} %copy-done.11, bf16[80,8,256]{2,1,0:T(8,128)(2,1)} %copy-done.16, bf16[80,8,256]{2,1,0:T(8,128)(2,1)} %copy-done.17, ...), custom_call_target="tpu_custom_call", output_to_operand_aliasing={{}: (8, {})} | custom-call | flops 4000000000 | bytes 10485760 | tf_op jit(solution)/shard_map/smooth/pallas_call | solution.py:165
  (63 shorter events, 0.6 us)
Async XLA Ops:
  0.0 1.4 copy-start.3
  1.4 0.7 copy-start.4
  2.1 0.7 copy-start.5
  49.9 33.6 %copy-start.18 = (f32[64,80]{1,0:T(8,128)S(1)}, f32[64,80]{1,0:T(8,128)}, u32[]{:S(2)}) copy-start(f32[64,80]{1,0:T(8,128)} %constant.18.clone) | copy-start | bytes 61444
  49.9 33.8 %copy-start.19 = (f32[80,64]{1,0:T(8,128)S(1)}, f32[80,64]{1,0:T(8,128)}, u32[]{:S(2)}) copy-start(f32[80,64]{1,0:T(8,128)} %constant.19.clone) | copy-start | bytes 61444
  49.9 29.4 %all-to-all-start.3 = ((bf16[32,64,256]{2,1,0:T(8,128)(2,1)}), bf16[32,64,256]{2,1,0:T(8,128)(2,1)S(1)}, u32[]{:S(2)}, u32[]{:S(2)}) async-start(bf16[32,64,256]{2,1,0:T(8,128)(2,1)} %bitcast.12), calls=%async_computation.3 | async-start | bytes 2097152 | tf_op jit(solution)/shard_map/all_to_all | solution.py:232
  54.6 8.4 %collective-permute-start.4 = (f32[8,64]{0,1:T(8,128)S(1)}, f32[8,64]{0,1:T(8,128)S(1)}, u32[]{:S(2)}, u32[]{:S(2)}) collective-permute-start(f32[8,64]{0,1:T(8,128)S(1)} %get-tuple-element.46), channel_id=1, source_target_pairs={{0,4},{4,8},{8,12},{12,16},{16,20},{20,24},{24,28},{1,5},{5,9},{9,... | collective-permute-start | bytes 6152 | tf_op jit(solution)/shard_map/ppermute | solution.py:203
  56.7 6.3 %collective-permute-start.5 = (f32[8,64]{0,1:T(8,128)S(1)}, f32[8,64]{0,1:T(8,128)S(1)}, u32[]{:S(2)}, u32[]{:S(2)}) collective-permute-start(f32[8,64]{0,1:T(8,128)S(1)} %get-tuple-element.47), channel_id=1, source_target_pairs={{4,0},{8,4},{12,8},{16,12},{20,16},{24,20},{28,24},{5,1},{9,5},{13... | collective-permute-start | bytes 6152 | tf_op jit(solution)/shard_map/ppermute | solution.py:204
  63.1 20.4 %collective-permute-start.6 = (f32[80,8]{0,1:T(8,128)S(1)}, f32[80,8]{0,1:T(8,128)S(1)}, u32[]{:S(2)}, u32[]{:S(2)}) collective-permute-start(f32[80,8]{0,1:T(8,128)S(1)} %pad_maximum_fusion.6), channel_id=1, source_target_pairs={{0,1},{1,2},{2,3},{4,5},{5,6},{6,7},{8,9},{9,10},{10,11},{12,13},{... | collective-permute-start | bytes 7688 | tf_op jit(solution)/shard_map/ppermute | solution.py:210
  66.4 17.1 %collective-permute-start.7 = (f32[80,8]{0,1:T(8,128)S(1)}, f32[80,8]{0,1:T(8,128)S(1)}, u32[]{:S(2)}, u32[]{:S(2)}) collective-permute-start(f32[80,8]{0,1:T(8,128)S(1)} %pad_maximum_fusion.7), channel_id=1, source_target_pairs={{1,0},{2,1},{3,2},{5,4},{6,5},{7,6},{9,8},{10,9},{11,10},{13,12},{... | collective-permute-start | bytes 7688 | tf_op jit(solution)/shard_map/ppermute | solution.py:211
  79.4 35.4 %all-to-all-start.1 = ((bf16[32,64,256]{2,1,0:T(8,128)(2,1)}), bf16[32,64,256]{2,1,0:T(8,128)(2,1)S(1)}, u32[]{:S(2)}, u32[]{:S(2)}) async-start(bf16[32,64,256]{2,1,0:T(8,128)(2,1)} %bitcast.2), calls=%async_computation.1 | async-start | bytes 2097152 | tf_op jit(solution)/shard_map/all_to_all | solution.py:232
  89.7 2.0 %copy-start = (f32[4096,256]{1,0:T(8,128)}, f32[4096,256]{1,0:T(8,128)S(1)}, u32[]{:S(2)}) copy-start(f32[4096,256]{1,0:T(8,128)S(1)} %accumulate.5) | copy-start | bytes 12582916
  92.9 31.7 %collective-permute-start.12 = (bf16[8,64,256]{2,1,0:T(8,128)(2,1)}, bf16[8,64,256]{2,1,0:T(8,128)(2,1)S(1)}, u32[]{:S(2)}, u32[]{:S(2)}) collective-permute-start(bf16[8,64,256]{2,1,0:T(8,128)(2,1)} %bitcast.15), channel_id=1, source_target_pairs={{0,4},{4,8},{8,12},{12,16},{16,20},{20,24},{24,28},{1,5},{5,9},{9,... | collective-permute-start | bytes 786440 | tf_op jit(solution)/shard_map/ppermute | solution.py:203
  95.0 34.2 %collective-permute-start.13 = (bf16[8,64,256]{2,1,0:T(8,128)(2,1)}, bf16[8,64,256]{2,1,0:T(8,128)(2,1)S(1)}, u32[]{:S(2)}, u32[]{:S(2)}) collective-permute-start(bf16[8,64,256]{2,1,0:T(8,128)(2,1)} %bitcast.16), channel_id=1, source_target_pairs={{4,0},{8,4},{12,8},{16,12},{20,16},{24,20},{28,24},{5,1},{9,5},{13... | collective-permute-start | bytes 786440 | tf_op jit(solution)/shard_map/ppermute | solution.py:204
  105.1 2.0 %copy-start.1 = (f32[4096,256]{1,0:T(8,128)}, f32[4096,256]{1,0:T(8,128)S(1)}, u32[]{:S(2)}) copy-start(f32[4096,256]{1,0:T(8,128)S(1)} %accumulate.4) | copy-start | bytes 12582916
  108.2 24.6 %collective-permute-start.8 = (bf16[8,64,256]{2,1,0:T(8,128)(2,1)}, bf16[8,64,256]{2,1,0:T(8,128)(2,1)S(1)}, u32[]{:S(2)}, u32[]{:S(2)}) collective-permute-start(bf16[8,64,256]{2,1,0:T(8,128)(2,1)} %bitcast.10), channel_id=1, source_target_pairs={{0,4},{4,8},{8,12},{12,16},{16,20},{20,24},{24,28},{1,5},{5,9},{9,... | collective-permute-start | bytes 786440 | tf_op jit(solution)/shard_map/ppermute | solution.py:203
  110.1 25.2 %collective-permute-start.9 = (bf16[8,64,256]{2,1,0:T(8,128)(2,1)S(1)}, bf16[8,64,256]{2,1,0:T(8,128)(2,1)S(1)}, u32[]{:S(2)}, u32[]{:S(2)}) collective-permute-start(bf16[8,64,256]{2,1,0:T(8,128)(2,1)S(1)} %bitcast.32), channel_id=1, source_target_pairs={{4,0},{8,4},{12,8},{16,12},{20,16},{24,20},{28,24},{5,1},{9,5},{13... | collective-permute-start | bytes 786440 | tf_op jit(solution)/shard_map/ppermute | solution.py:204
  120.5 2.0 copy-start.2
  122.7 16.1 %collective-permute-start = (bf16[8,64,256]{2,1,0:T(8,128)(2,1)S(1)}, bf16[8,64,256]{2,1,0:T(8,128)(2,1)S(1)}, u32[]{:S(2)}, u32[]{:S(2)}) collective-permute-start(bf16[8,64,256]{2,1,0:T(8,128)(2,1)S(1)} %bitcast.34), channel_id=1, source_target_pairs={{0,4},{4,8},{8,12},{12,16},{16,20},{20,24},{24,28},{1,5},{5,9},{9,... | collective-permute-start | bytes 786440 | tf_op jit(solution)/shard_map/ppermute | solution.py:203
  124.7 20.2 %copy-start.6 = (bf16[8,64,256]{2,1,0:T(8,128)(2,1)}, bf16[8,64,256]{2,1,0:T(8,128)(2,1)S(1)}, u32[]{:S(2)}) copy-start(bf16[8,64,256]{2,1,0:T(8,128)(2,1)S(1)} %collective-permute-done.12.top_ref) | copy-start | bytes 786436
  124.7 16.7 %collective-permute-start.1 = (bf16[8,64,256]{2,1,0:T(8,128)(2,1)S(1)}, bf16[8,64,256]{2,1,0:T(8,128)(2,1)S(1)}, u32[]{:S(2)}, u32[]{:S(2)}) collective-permute-start(bf16[8,64,256]{2,1,0:T(8,128)(2,1)S(1)} %bitcast.33), channel_id=1, source_target_pairs={{4,0},{8,4},{12,8},{16,12},{20,16},{24,20},{28,24},{5,1},{9,5},{13... | collective-permute-start | bytes 786440 | tf_op jit(solution)/shard_map/ppermute | solution.py:204
  129.2 15.6 %copy-start.8 = (bf16[8,64,256]{2,1,0:T(8,128)(2,1)}, bf16[8,64,256]{2,1,0:T(8,128)(2,1)S(1)}, u32[]{:S(2)}) copy-start(bf16[8,64,256]{2,1,0:T(8,128)(2,1)S(1)} %collective-permute-done.13.bot_ref) | copy-start | bytes 786436
  129.3 15.5 %collective-permute-start.14 = (bf16[80,8,256]{2,1,0:T(8,128)(2,1)S(1)}, bf16[80,8,256]{2,1,0:T(8,128)(2,1)S(1)}, u32[]{:S(2)}, u32[]{:S(2)}) collective-permute-start(bf16[80,8,256]{2,1,0:T(8,128)(2,1)S(1)} %pad_maximum_fusion.4), channel_id=1, source_target_pairs={{0,1},{1,2},{2,3},{4,5},{5,6},{6,7},{8,9},{9,10},{10,11},{12,13},{... | collective-permute-start | bytes 983048 | tf_op jit(solution)/shard_map/ppermute | solution.py:210
  132.8 16.5 %copy-start.7 = (bf16[8,64,256]{2,1,0:T(8,128)(2,1)}, bf16[8,64,256]{2,1,0:T(8,128)(2,1)S(1)}, u32[]{:S(2)}) copy-start(bf16[8,64,256]{2,1,0:T(8,128)(2,1)S(1)} %collective-permute-done.8.top_ref) | copy-start | bytes 786436
  132.8 14.6 %collective-permute-start.15 = (bf16[80,8,256]{2,1,0:T(8,128)(2,1)S(1)}, bf16[80,8,256]{2,1,0:T(8,128)(2,1)S(1)}, u32[]{:S(2)}, u32[]{:S(2)}) collective-permute-start(bf16[80,8,256]{2,1,0:T(8,128)(2,1)S(1)} %pad_maximum_fusion.5), channel_id=1, source_target_pairs={{1,0},{2,1},{3,2},{5,4},{6,5},{7,6},{9,8},{10,9},{11,10},{13,12},{... | collective-permute-start | bytes 983048 | tf_op jit(solution)/shard_map/ppermute | solution.py:211
  135.3 14.0 %copy-start.9 = (bf16[8,64,256]{2,1,0:T(8,128)(2,1)}, bf16[8,64,256]{2,1,0:T(8,128)(2,1)S(1)}, u32[]{:S(2)}) copy-start(bf16[8,64,256]{2,1,0:T(8,128)(2,1)S(1)} %collective-permute-done.9.bot_ref) | copy-start | bytes 786436
  135.4 30.1 %collective-permute-start.10 = (bf16[80,8,256]{2,1,0:T(8,128)(2,1)S(1)}, bf16[80,8,256]{2,1,0:T(8,128)(2,1)S(1)}, u32[]{:S(2)}, u32[]{:S(2)}) collective-permute-start(bf16[80,8,256]{2,1,0:T(8,128)(2,1)S(1)} %pad_maximum_fusion.2), channel_id=1, source_target_pairs={{0,1},{1,2},{2,3},{4,5},{5,6},{6,7},{8,9},{9,10},{10,11},{12,13},{... | collective-permute-start | bytes 983048 | tf_op jit(solution)/shard_map/ppermute | solution.py:210
  138.8 26.6 %copy-start.10 = (bf16[8,64,256]{2,1,0:T(8,128)(2,1)}, bf16[8,64,256]{2,1,0:T(8,128)(2,1)S(1)}, u32[]{:S(2)}) copy-start(bf16[8,64,256]{2,1,0:T(8,128)(2,1)S(1)} %collective-permute-done.top_ref) | copy-start | bytes 786436
  138.8 26.6 %collective-permute-start.11 = (bf16[80,8,256]{2,1,0:T(8,128)(2,1)S(1)}, bf16[80,8,256]{2,1,0:T(8,128)(2,1)S(1)}, u32[]{:S(2)}, u32[]{:S(2)}) collective-permute-start(bf16[80,8,256]{2,1,0:T(8,128)(2,1)S(1)} %pad_maximum_fusion.3), channel_id=1, source_target_pairs={{1,0},{2,1},{3,2},{5,4},{6,5},{7,6},{9,8},{10,9},{11,10},{13,12},{... | collective-permute-start | bytes 983048 | tf_op jit(solution)/shard_map/ppermute | solution.py:211
  141.3 24.1 %copy-start.11 = (bf16[8,64,256]{2,1,0:T(8,128)(2,1)}, bf16[8,64,256]{2,1,0:T(8,128)(2,1)S(1)}, u32[]{:S(2)}) copy-start(bf16[8,64,256]{2,1,0:T(8,128)(2,1)S(1)} %collective-permute-done.1.bot_ref) | copy-start | bytes 786436
  141.4 41.6 %collective-permute-start.2 = (bf16[80,8,256]{2,1,0:T(8,128)(2,1)S(1)}, bf16[80,8,256]{2,1,0:T(8,128)(2,1)S(1)}, u32[]{:S(2)}, u32[]{:S(2)}) collective-permute-start(bf16[80,8,256]{2,1,0:T(8,128)(2,1)S(1)} %pad_maximum_fusion), channel_id=1, source_target_pairs={{0,1},{1,2},{2,3},{4,5},{5,6},{6,7},{8,9},{9,10},{10,11},{12,13},{... | collective-permute-start | bytes 983048 | tf_op jit(solution)/shard_map/ppermute | solution.py:210
  144.9 4.5 %copy-start.12 = (bf16[80,8,256]{2,1,0:T(8,128)(2,1)}, bf16[80,8,256]{2,1,0:T(8,128)(2,1)S(1)}, u32[]{:S(2)}) copy-start(bf16[80,8,256]{2,1,0:T(8,128)(2,1)S(1)} %collective-permute-done.14.left_ref) | copy-start | bytes 983044
  144.9 38.1 %collective-permute-start.3 = (bf16[80,8,256]{2,1,0:T(8,128)(2,1)S(1)}, bf16[80,8,256]{2,1,0:T(8,128)(2,1)S(1)}, u32[]{:S(2)}, u32[]{:S(2)}) collective-permute-start(bf16[80,8,256]{2,1,0:T(8,128)(2,1)S(1)} %pad_maximum_fusion.1), channel_id=1, source_target_pairs={{1,0},{2,1},{3,2},{5,4},{6,5},{7,6},{9,8},{10,9},{11,10},{13,12},{... | collective-permute-start | bytes 983048 | tf_op jit(solution)/shard_map/ppermute | solution.py:211
  147.4 1.9 copy-start.13
  165.4 0.8 copy-start.14
  166.2 0.7 copy-start.15
  183.0 0.7 copy-start.16
  183.7 0.7 copy-start.17
